TPU v7x, 512 devices: a whole 4x4x16 slice. The times are simulated.
512 devices in a mesh: rows: 32 (over z_lo, y, core), gz: 16 (over z_hi, x).
Axes of the slice: x: 4, y: 4, z: 16 (z_hi: 4, z_lo: 4; z = z_hi * 4 + z_lo), core: 2. Of those that a mesh axis runs over, the one named last changes fastest.
Arguments:
- plane_colour_samples: int32 [32, 3, 1024, 2048], P('gz', None, 'rows'), may hold values from 0 to 255
- clarity_gain: float32 [32], P('gz'), may hold values from 0.01 to 4
Outputs:
- joined: float32 [3, 1024, 2048], P(None, 'rows')
All inputs are finite; a program needn't handle non-finite values.
Results may differ from a plain program's by a relative error of at most 0.000067.
Values sent between devices are 32-bit elements; how exact they have to be, the bound alone decides.
No kernel may reach another device: no remote copies, remote signals or barrier semaphores. Data moves between devices by JAX's collectives and lax.ppermute only.
A program may use at most 64 MiB of HBM per device.

v0:
```python
import jax
import jax.numpy as jnp
from jax import lax
from jax.sharding import PartitionSpec as P


def extended(block, sides, width):
    for axis, dim in sides:
        count = lax.axis_size(axis)
        forward = [(i, i + 1) for i in range(count - 1)]
        backward = [(target, source) for source, target in forward]
        low = lax.ppermute(
            lax.slice_in_dim(block, block.shape[dim] - width, None, axis=dim), axis, forward
        )
        high = lax.ppermute(lax.slice_in_dim(block, 0, width, axis=dim), axis, backward)
        block = jnp.concatenate([low, block, high], axis=dim)
    return block


def blur_rows(padded_image, count):
    return (
        padded_image[..., 0:count, :]
        + 4.0 * padded_image[..., 1 : count + 1, :]
        + 6.0 * padded_image[..., 2 : count + 2, :]
        + 4.0 * padded_image[..., 3 : count + 3, :]
        + padded_image[..., 4 : count + 4, :]
    ) / 16.0


def blur_cols(field):
    count = field.shape[-1]
    padded_image = jnp.pad(field, [(0, 0)] * (field.ndim - 1) + [(2, 2)])
    return (
        padded_image[..., 0:count]
        + 4.0 * padded_image[..., 1 : count + 1]
        + 6.0 * padded_image[..., 2 : count + 2]
        + 4.0 * padded_image[..., 3 : count + 3]
        + padded_image[..., 4 : count + 4]
    ) / 16.0


def upsampled_rows(padded_image, count):
    even = (
        padded_image[..., 0:count, :]
        + 6.0 * padded_image[..., 1 : count + 1, :]
        + padded_image[..., 2 : count + 2, :]
    ) / 8.0
    odd = (padded_image[..., 1 : count + 1, :] + padded_image[..., 2 : count + 2, :]) / 2.0
    shape = even.shape[:-2] + (2 * count, even.shape[-1])
    return jnp.stack([even, odd], axis=-2).reshape(shape)


def up_cols(field):
    count = field.shape[-1]
    padded_image = jnp.pad(field, [(0, 0)] * (field.ndim - 1) + [(1, 1)])
    even = (
        padded_image[..., 0:count]
        + 6.0 * padded_image[..., 1 : count + 1]
        + padded_image[..., 2 : count + 2]
    ) / 8.0
    odd = (padded_image[..., 1 : count + 1] + padded_image[..., 2 : count + 2]) / 2.0
    shape = field.shape[:-1] + (2 * count,)
    return jnp.stack([even, odd], axis=-1).reshape(shape)


def reduce_level(padded_image, count):
    return blur_cols(blur_rows(padded_image, count))[..., ::2, ::2]


def expand_level(padded_image, count):
    return up_cols(upsampled_rows(padded_image, count))


def octave_border(field):
    return extended(field, (("rows", 2),), 2)


def collapse(mixed_finest_band, mixed_coarse_band, blend2, strip):
    central_rows = mixed_coarse_band + expand_level(octave_border(blend2)[..., 1:-1, :], strip // 4)
    return mixed_finest_band + expand_level(octave_border(central_rows)[..., 1:-1, :], strip // 2)


def on_device(plane_colour_samples, clarity_gain):
    strip = plane_colour_samples.shape[2]
    image = plane_colour_samples.astype(jnp.float32) / 255.0
    padded_image = extended(image, (("rows", 2),), 5)
    grey = 0.299 * padded_image[:, 0] + 0.587 * padded_image[:, 1] + 0.114 * padded_image[:, 2]
    side = jnp.pad(grey, ((0, 0), (0, 0), (1, 1)))
    lap = (
        4.0 * grey[:, 1:-1, :]
        - grey[:, :-2, :]
        - grey[:, 2:, :]
        - side[:, 1:-1, :-2]
        - side[:, 1:-1, 2:]
    )
    height = strip * lax.axis_size("rows")
    first_row = lax.axis_index("rows") * strip - 4
    line_slice_from = first_row + jnp.arange(strip + 8, dtype=jnp.int32)
    inside = ((line_slice_from >= 0) & (line_slice_from < height)).astype(jnp.float32)
    squared = lap * lap * inside[None, :, None]
    summed = squared[:, 0:strip]
    for shift in range(1, 9):
        summed = summed + squared[:, shift : shift + strip]
    width = summed.shape[2]
    cols_pad = jnp.pad(summed, ((0, 0), (0, 0), (4, 4)))
    sharpness_measure_field = cols_pad[:, :, 0:width]
    for shift in range(1, 9):
        sharpness_measure_field = sharpness_measure_field + cols_pad[:, :, shift : shift + width]
    clarity_ratings = clarity_gain[:, None, None] * sharpness_measure_field
    top = lax.pmax(jnp.max(clarity_ratings, axis=0), "gz")
    expo = jnp.exp(clarity_ratings - top[None])
    total = lax.psum(jnp.sum(expo, axis=0), "gz")
    weight0 = (expo / total[None])[:, None]
    level1 = reduce_level(padded_image[..., 3:-3, :], strip)
    level1_pad = octave_border(level1)
    level2 = reduce_level(level1_pad, strip // 2)
    padded_level_second = octave_border(level2)
    detail0 = image - expand_level(level1_pad[..., 1:-1, :], strip // 2)
    detail1 = level1 - expand_level(padded_level_second[..., 1:-1, :], strip // 4)
    weight1 = reduce_level(octave_border(weight0), strip)
    weight_level2 = reduce_level(octave_border(weight1), strip // 2)
    mixed_finest_band = jnp.sum(weight0 * detail0, axis=0, keepdims=True)
    mixed_coarse_band = jnp.sum(weight1 * detail1, axis=0, keepdims=True)
    blend2 = jnp.sum(weight_level2 * level2, axis=0, keepdims=True)
    mixed_finest_band, mixed_coarse_band, blend2 = lax.psum(
        (mixed_finest_band, mixed_coarse_band, blend2), "gz"
    )
    joined = collapse(mixed_finest_band, mixed_coarse_band, blend2, strip)
    return joined[0]


def solution(mesh):
    placed = (P("gz", None, "rows", None), P("gz"))
    return jax.shard_map(
        on_device, mesh=mesh, in_specs=placed, out_specs=P(None, "rows", None), check_vma=False
    )
```

profile of v0, /device:TPU:1, one launch (start us, length us, event | category | flops | bytes accessed | tf_op | source)
XLA Modules:
  0.0 865.2 jit_solution(9867116555211420040)
XLA Ops:
  6.5 1.6 convert_multiply_fusion
  8.4 8.8 %collective-permute-start.1 = (f32[2,3,5,2048]{3,0,2,1:T(2,128)S(1)}, f32[2,3,5,2048]{3,0,2,1:T(2,128)S(1)}, u32[]{:S(2)}, u32[]{:S(2)}) collective-permute-start(f32[2,3,5,2048]{3,0,2,1:T(2,128)S(1)} %copy.379), channel_id=1, source_target_pairs={{16,0},{32,16},{48,32},{64,48},{80,64},{96,80},{112,96},{128,112},... | collective-permute-start | bytes 737288 | tf_op jit(solution)/shard_map/ppermute | solution.py:15
  17.4 1.9 collective-permute-start
  19.5 2.9 collective-permute-done
  23.0 1.0 copy-done
  24.0 1.0 broadcast_multiply_fusion
  25.2 0.4 fusion.18
  25.7 1.2 slice_add_fusion
  26.8 1.7 add_multiply_fusion
  28.5 17.7 %slice.380 = f32[2,3,16,1024]{3,2,1,0:T(8,128)S(1)} slice(f32[2,3,32,2048]{3,2,1,0:T(8,128)S(1)} %add_multiply_fusion), slice={[0:2:1], [0:3:1], [0:32:2], [0:2048:2]} | slice | bytes 786432 | tf_op jit(solution)/shard_map/slice | solution.py:67
  46.3 4.4 collective-permute-start.2
  50.7 1.9 collective-permute-start.3
  52.6 4.9 fusion.74
  58.1 1.2 fusion.35
  59.4 4.3 slice.404
  63.7 0.7 fusion.80
  64.3 3.6 collective-permute-start.6
  68.0 1.9 collective-permute-start.7
  70.0 1.5 copy.384
  71.5 181.4 %all-reduce.15.cloned.1.call-done = f32[32,2048]{1,0:T(8,128)} async-done(((f32[32,2048]{1,0:T(8,128)}), f32[32,2048]{1,0:T(8,128)}) %all-reduce.15.cloned.1.call-update) | async-done | bytes 262160 | tf_op jit(solution)/shard_map/pmax | solution.py:110
  252.9 1.8 fusion.30
  254.8 2.5 multiply_bitcast_fusion.2
  257.3 2.0 pad_maximum_fusion.3
  259.2 9.2 %copy.387 = f32[2,3,32,1024,2]{2,4,3,1,0:T(2,128)} copy(f32[2,3,32,1024,2]{3,0,2,1,4:T(2,128)} %pad_maximum_fusion.3) | data formatting | bytes 3145728 | tf_op jit(solution)/shard_map/stack | solution.py:63
  268.4 5.6 copy.388
  274.0 183.3 %all-reduce.17.cloned.1.call-done = f32[32,2048]{1,0:T(8,128)} async-done(((f32[32,2048]{1,0:T(8,128)}), f32[32,2048]{1,0:T(8,128)}) %all-reduce.17.cloned.1.call-update) | async-done | bytes 262160 | tf_op jit(solution)/shard_map/psum | solution.py:112
  457.3 1.1 fusion.81
  458.5 14.3 %collective-permute-start.4 = (f32[2,1,2,2048]{3,2,1,0:T(2,128)S(1)}, f32[2,1,2,2048]{3,2,1,0:T(2,128)S(1)}, u32[]{:S(2)}, u32[]{:S(2)}) collective-permute-start(f32[2,1,2,2048]{3,2,1,0:T(2,128)S(1)} %get-tuple-element.25), channel_id=1, source_target_pairs={{0,16},{16,32},{32,48},{48,64},{64,80},{80,96},{96,112},{112,128},... | collective-permute-start | bytes 98312 | tf_op jit(solution)/shard_map/ppermute | solution.py:12
  472.8 2.1 collective-permute-start.5
  474.9 0.9 fusion.29
  475.9 2.1 collective-permute-done.5
  478.0 0.4 broadcast_multiply_fusion.1
  478.4 1.4 add_multiply_fusion.1
  479.8 6.0 slice.397
  485.9 0.9 slice_bitcast_fusion.3
  486.8 1.9 collective-permute-start.8
  488.7 2.5 collective-permute-start.9
  491.2 2.4 multiply_reduce_fusion
  494.2 1.1 slice.421
  495.4 1.1 fusion.69
  496.7 0.7 multiply_bitcast_fusion.8
  497.6 110.6 %psum.31 = f32[1,3,8,512]{2,3,1,0:T(8,128)} all-reduce(f32[1,3,8,512]{2,3,1,0:T(8,128)S(1)} %bitcast.84), channel_id=1, replica_groups=mesh['rows'=32,'gz'=16] {'gz'}, use_global_device_ids=true, to_apply=%region_9.10 | all-reduce | flops 12288 | bytes 98304 | tf_op jit(solution)/shard_map/psum | solution.py:125
  608.3 0.9 pad_maximum_fusion.13
  609.2 3.5 copy.396
  612.7 1.8 copy.397
  614.5 1.9 multiply_reduce_fusion.1
  617.0 12.2 %collective-permute-start.10 = (f32[1,3,2,512]{3,2,1,0:T(2,128)S(1)}, f32[1,3,2,512]{3,2,1,0:T(2,128)S(1)}, u32[]{:S(2)}, u32[]{:S(2)}) collective-permute-start(f32[1,3,2,512]{3,2,1,0:T(2,128)S(1)} %copy.407), channel_id=1, source_target_pairs={{0,16},{16,32},{32,48},{48,64},{64,80},{80,96},{96,112},{112,128},... | collective-permute-start | bytes 36872 | tf_op jit(solution)/shard_map/ppermute | solution.py:12
  629.4 2.2 collective-permute-start.11
  631.9 2.5 collective-permute-done.11
  634.7 0.9 fusion.11
  635.7 0.4 copy.411
  636.1 0.7 multiply_bitcast_fusion.10
  637.0 0.8 copy.413
  637.8 0.4 copy.414
  638.2 188.5 %all-reduce.19.cloned.1.call-done = (f32[1,3,32,2048]{3,2,1,0:T(8,128)}, f32[1,3,16,1024]{3,2,1,0:T(8,128)}) async-done(((f32[1,3,32,2048]{3,2,1,0:T(8,128)}, f32[1,3,16,1024]{3,2,1,0:T(8,128)}), (f32[1,3,32,2048]{3,2,1,0:T(8,128)}, f32[1,3,16,1024]{3,2,1,0:T(8,128)})) %all-reduce.19.cloned.1.call-update) | async-done | bytes 983056 | tf_op jit(solution)/shard_map/psum | solution.py:125
  826.7 0.9 add.342
  827.7 13.3 %collective-permute-start.12 = (f32[1,3,2,1024]{3,2,1,0:T(2,128)S(1)}, f32[1,3,2,1024]{3,2,1,0:T(2,128)S(1)}, u32[]{:S(2)}, u32[]{:S(2)}) collective-permute-start(f32[1,3,2,1024]{3,2,1,0:T(2,128)S(1)} %get-tuple-element.35), channel_id=1, source_target_pairs={{0,16},{16,32},{32,48},{48,64},{64,80},{80,96},{96,112},{112,128},... | collective-permute-start | bytes 73736 | tf_op jit(solution)/shard_map/ppermute | solution.py:12
  840.9 1.9 collective-permute-start.13
  842.9 3.2 collective-permute-done.13
  846.6 2.5 multiply_bitcast_fusion.4
  849.1 1.7 pad_maximum_fusion.8
  850.8 3.7 copy.417
  854.5 1.9 copy.418
  856.4 2.3 add_bitcast_fusion
  (61 shorter events, 5.3 us)
Async XLA Ops:
  6.5 246.4 %all-reduce.15.cloned.1.call-start = ((), (), s32[]{:S(2)}) async-start(), calls=%async_computation | async-start | bytes 524288 | tf_op jit(solution)/shard_map/pmax | solution.py:110
  8.4 10.9 %collective-permute-start.1 = (f32[2,3,5,2048]{3,0,2,1:T(2,128)S(1)}, f32[2,3,5,2048]{3,0,2,1:T(2,128)S(1)}, u32[]{:S(2)}, u32[]{:S(2)}) collective-permute-start(f32[2,3,5,2048]{3,0,2,1:T(2,128)S(1)} %copy.379), channel_id=1, source_target_pairs={{16,0},{32,16},{48,32},{64,48},{80,64},{96,80},{112,96},{128,112},... | collective-permute-start | bytes 737288 | tf_op jit(solution)/shard_map/ppermute | solution.py:15
  17.4 5.0 collective-permute-start
  22.6 1.4 copy-start
  26.8 25.8 %copy-start.8 = (f32[2]{0:T(128)S(1)}, f32[2]{0:T(128)}, u32[]{:S(2)}) copy-start(f32[2]{0:T(128)} %param.3) | copy-start | bytes 28
  46.3 11.5 %collective-permute-start.2 = (f32[2,3,2,1024]{3,2,1,0:T(2,128)S(1)}, f32[2,3,2,1024]{3,2,1,0:T(2,128)S(1)}, u32[]{:S(2)}, u32[]{:S(2)}) collective-permute-start(f32[2,3,2,1024]{3,2,1,0:T(2,128)S(1)} %get-tuple-element.31), channel_id=1, source_target_pairs={{0,16},{16,32},{32,48},{48,64},{64,80},{80,96},{96,112},{112,128},... | collective-permute-start | bytes 147464 | tf_op jit(solution)/shard_map/ppermute | solution.py:12
  50.7 7.1 collective-permute-start.3
  57.5 399.8 %all-reduce.17.cloned.1.call-start = ((), (), s32[]{:S(2)}) async-start(), calls=%async_computation.1 | async-start | bytes 524288 | tf_op jit(solution)/shard_map/psum | solution.py:112
  63.7 7.8 copy-start.7
  64.3 431.0 %collective-permute-start.6 = (f32[2,3,2,512]{3,2,1,0:T(2,128)}, f32[2,3,2,512]{3,2,1,0:T(2,128)}, u32[]{:S(2)}, u32[]{:S(2)}) collective-permute-start(f32[2,3,2,512]{3,2,1,0:T(2,128)} %get-tuple-element.46), channel_id=1, source_target_pairs={{0,16},{16,32},{32,48},{48,64},{64,80},{80,96},{96,112},{112,128},... | collective-permute-start | bytes 73736 | tf_op jit(solution)/shard_map/ppermute | solution.py:12
  68.0 427.4 %collective-permute-start.7 = (f32[2,3,2,512]{3,2,1,0:T(2,128)}, f32[2,3,2,512]{3,2,1,0:T(2,128)}, u32[]{:S(2)}, u32[]{:S(2)}) collective-permute-start(f32[2,3,2,512]{3,2,1,0:T(2,128)} %get-tuple-element.47), channel_id=1, source_target_pairs={{16,0},{32,16},{48,32},{64,48},{80,64},{96,80},{112,96},{128,112},... | collective-permute-start | bytes 73736 | tf_op jit(solution)/shard_map/ppermute | solution.py:15
  71.5 183.3 %copy-start.4 = (f32[2,3,16,2,1024]{4,0,3,2,1:T(2,128)S(1)}, f32[2,3,16,2,1024]{4,0,3,2,1:T(2,128)}, u32[]{:S(2)}) copy-start(f32[2,3,16,2,1024]{4,0,3,2,1:T(2,128)} %copy.384) | copy-start | bytes 2359300
  254.7 572.0 %all-reduce.19.cloned.1.call-start = ((), (), s32[]{:S(2)}) async-start(), calls=%async_computation.2 | async-start | bytes 1966080 | tf_op jit(solution)/shard_map/psum | solution.py:125
  268.4 188.9 %copy-start.3 = (f32[32,2048]{1,0:T(8,128)S(1)}, f32[32,2048]{1,0:T(8,128)}, u32[]{:S(2)}) copy-start(f32[32,2048]{1,0:T(8,128)} %all-reduce.15.cloned.1.call-done) | copy-start | bytes 786436
  457.3 17.6 %copy-start.5 = (f32[32,2048]{1,0:T(8,128)S(1)}, f32[32,2048]{1,0:T(8,128)}, u32[]{:S(2)}) copy-start(f32[32,2048]{1,0:T(8,128)} %all-reduce.17.cloned.1.call-done) | copy-start | bytes 786436
  458.5 17.4 %collective-permute-start.4 = (f32[2,1,2,2048]{3,2,1,0:T(2,128)S(1)}, f32[2,1,2,2048]{3,2,1,0:T(2,128)S(1)}, u32[]{:S(2)}, u32[]{:S(2)}) collective-permute-start(f32[2,1,2,2048]{3,2,1,0:T(2,128)S(1)} %get-tuple-element.25), channel_id=1, source_target_pairs={{0,16},{16,32},{32,48},{48,64},{64,80},{80,96},{96,112},{112,128},... | collective-permute-start | bytes 98312 | tf_op jit(solution)/shard_map/ppermute | solution.py:12
  472.8 5.2 collective-permute-start.5
  478.4 12.8 %copy-start.2 = (f32[2,3,32,2048]{3,2,1,0:T(8,128)S(1)}, f32[2,3,32,2048]{3,2,1,0:T(8,128)}, u32[]{:S(2)}) copy-start(f32[2,3,32,2048]{3,2,1,0:T(8,128)} %copy.388) | copy-start | bytes 4718596
  486.8 6.9 collective-permute-start.8
  488.7 5.2 copy-start.6
  488.7 5.2 collective-permute-start.9
  614.5 1.9 copy-start.1
  617.0 14.6 %collective-permute-start.10 = (f32[1,3,2,512]{3,2,1,0:T(2,128)S(1)}, f32[1,3,2,512]{3,2,1,0:T(2,128)S(1)}, u32[]{:S(2)}, u32[]{:S(2)}) collective-permute-start(f32[1,3,2,512]{3,2,1,0:T(2,128)S(1)} %copy.407), channel_id=1, source_target_pairs={{0,16},{16,32},{32,48},{48,64},{64,80},{80,96},{96,112},{112,128},... | collective-permute-start | bytes 36872 | tf_op jit(solution)/shard_map/ppermute | solution.py:12
  629.4 5.0 collective-permute-start.11
  827.7 15.2 %collective-permute-start.12 = (f32[1,3,2,1024]{3,2,1,0:T(2,128)S(1)}, f32[1,3,2,1024]{3,2,1,0:T(2,128)S(1)}, u32[]{:S(2)}, u32[]{:S(2)}) collective-permute-start(f32[1,3,2,1024]{3,2,1,0:T(2,128)S(1)} %get-tuple-element.35), channel_id=1, source_target_pairs={{0,16},{16,32},{32,48},{48,64},{64,80},{80,96},{96,112},{112,128},... | collective-permute-start | bytes 73736 | tf_op jit(solution)/shard_map/ppermute | solution.py:12
  840.9 5.1 collective-permute-start.13
Sparse Core Ops, SparseCore 0:
  57.7 195.2 all-reduce.14
  256.1 201.1 all-reduce.16
  616.5 210.0 all-reduce.18
where the time goes:
time: 867 us; the launch traced here: 865 us
  waiting for transfers between devices  564 us (65%)
  blocking collectives  111 us (13%)
  starting transfers between devices  73.2 us (8%)
  local copies, waits for them, and re-layouts  63.7 us (7%)
  other arithmetic  39.8 us (5%)
  between operations  13.6 us (2%)
    psum x1, waiting for transfers between devices, on_device(): lax.psum((mixed_finest_band, mixed_coarse_band, blend2), 'gz')  188 us
    psum x1, waiting for transfers between devices, on_device(): total = lax.psum(jnp.sum(expo, axis=0), 'gz')  183 us
    pmax x1, waiting for transfers between devices, on_device(): top = lax.pmax(jnp.max(clarity_ratings, axis=0), 'gz')  181 us
    psum x1, blocking collectives, on_device(): lax.psum((mixed_finest_band, mixed_coarse_band, blend2), 'gz')  111 us
    ppermute x7, starting transfers between devices, extended(): lax.ppermute(lax.slice_in_dim(block, block.shape[dim] - width, None, axis...  51.6 us
    slice x4, local copies, waits for them, and re-layouts, reduce_level(): return blur_cols(blur_rows(padded_image, count))[..., ::2, ::2]  29.2 us
    ppermute x7, starting transfers between devices, extended(): lax.ppermute(lax.slice_in_dim(block, 0, width, axis=dim), axis, backward)  21.4 us
  transfers between devices with their start and end apart: 17, of which 8 were waited for; matrix products, arithmetic and copies ran while one was open for 6% of the time, Pallas kernels for 0%

commit v1 on v0

--- a/solution.py
+++ b/solution.py
@@ -109,7 +109,9 @@
     clarity_ratings = clarity_gain[:, None, None] * sharpness_measure_field
     top = lax.pmax(jnp.max(clarity_ratings, axis=0), "gz")
     expo = jnp.exp(clarity_ratings - top[None])
-    total = lax.psum(jnp.sum(expo, axis=0), "gz")
+    own = jnp.sum(expo, axis=0)
+    parts = lax.all_gather(own, "gz", axis=0, tiled=False)
+    total = parts.sum(axis=0)
     weight0 = (expo / total[None])[:, None]
     level1 = reduce_level(padded_image[..., 3:-3, :], strip)
     level1_pad = octave_border(level1)

time: 867 us -> 761 us (0.88)
  waiting for transfers between devices: 564 us -> 476 us
  blocking collectives: 111 us -> 99 us
    psum x1 -> x0, waiting for transfers between devices: 183 us -> none  [on_device(): total = lax.psum(jnp.sum(expo, axis=0), 'gz')]
    all_gather x0 -> x1, waiting for transfers between devices: none -> 78.2 us  [on_device(): parts = lax.all_gather(own, 'gz', axis=0, tiled=False)]
    pmax x1, waiting for transfers between devices: 181 us -> 194 us  [on_device(): top = lax.pmax(jnp.max(clarity_ratings, axis=0), 'gz')]
    psum x1, blocking collectives: 111 us -> 99 us  [on_device(): lax.psum((mixed_finest_band, mixed_coarse_band, blend2), 'gz')]
  transfers between devices with their start and end apart: 17 -> 17, of which waited for: 8 -> 9; matrix products, arithmetic and copies ran while one was open for 6% -> 8% of each run, Pallas kernels for 0% -> 0%
where the time goes in v1:
time: 761 us; the launch traced here: 760 us
  waiting for transfers between devices  476 us (63%)
  blocking collectives  99 us (13%)
  starting transfers between devices  75.2 us (10%)
  local copies, waits for them, and re-layouts  59.2 us (8%)
  other arithmetic  37.5 us (5%)
  between operations  13.7 us (2%)
    pmax x1, waiting for transfers between devices, on_device(): top = lax.pmax(jnp.max(clarity_ratings, axis=0), 'gz')  194 us
    psum x1, waiting for transfers between devices, on_device(): lax.psum((mixed_finest_band, mixed_coarse_band, blend2), 'gz')  190 us
    psum x1, blocking collectives, on_device(): lax.psum((mixed_finest_band, mixed_coarse_band, blend2), 'gz')  99 us
    all_gather x1, waiting for transfers between devices, on_device(): parts = lax.all_gather(own, 'gz', axis=0, tiled=False)  78.2 us
    ppermute x7, starting transfers between devices, extended(): lax.ppermute(lax.slice_in_dim(block, block.shape[dim] - width, None, axis...  51.7 us
    slice x4, local copies, waits for them, and re-layouts, reduce_level(): return blur_cols(blur_rows(padded_image, count))[..., ::2, ::2]  28.4 us
    ppermute x7, starting transfers between devices, extended(): lax.ppermute(lax.slice_in_dim(block, 0, width, axis=dim), axis, backward)  23.4 us
  transfers between devices with their start and end apart: 17, of which 9 were waited for; matrix products, arithmetic and copies ran while one was open for 8% of the time, Pallas kernels for 0%

profile of v1, /device:TPU:1, one launch (start us, length us, event | category | flops | bytes accessed | tf_op | source)
XLA Modules:
  0.0 760.3 jit_solution(455375325038389405)
XLA Ops:
  6.5 1.6 convert_multiply_fusion
  8.4 8.8 %collective-permute-start.1 = (f32[2,3,5,2048]{3,0,2,1:T(2,128)S(1)}, f32[2,3,5,2048]{3,0,2,1:T(2,128)S(1)}, u32[]{:S(2)}, u32[]{:S(2)}) collective-permute-start(f32[2,3,5,2048]{3,0,2,1:T(2,128)S(1)} %copy.435), channel_id=1, source_target_pairs={{16,0},{32,16},{48,32},{64,48},{80,64},{96,80},{112,96},{128,112},... | collective-permute-start | bytes 737288 | tf_op jit(solution)/shard_map/ppermute | solution.py:15
  17.4 1.9 collective-permute-start
  19.5 2.9 collective-permute-done
  22.6 0.7 copy-done.5
  23.9 0.4 fusion.18
  24.9 2.7 fusion.74
  27.7 193.8 %all-reduce.14.cloned.1.call-done = f32[32,2048]{1,0:T(8,128)} async-done(((f32[32,2048]{1,0:T(8,128)}), f32[32,2048]{1,0:T(8,128)}) %all-reduce.14.cloned.1.call-update) | async-done | bytes 262160 | tf_op jit(solution)/shard_map/pmax | solution.py:110
  221.5 1.9 fusion.30
  223.5 2.2 broadcast_multiply_fusion
  225.7 1.7 add_multiply_fusion
  227.4 17.7 %slice.380 = f32[2,3,16,1024]{3,2,1,0:T(8,128)S(1)} slice(f32[2,3,32,2048]{3,2,1,0:T(8,128)S(1)} %add_multiply_fusion), slice={[0:2:1], [0:3:1], [0:32:2], [0:2048:2]} | slice | bytes 786432 | tf_op jit(solution)/shard_map/slice | solution.py:67
  245.1 14.3 %collective-permute-start.2 = (f32[2,3,2,1024]{3,2,1,0:T(2,128)S(1)}, f32[2,3,2,1024]{3,2,1,0:T(2,128)S(1)}, u32[]{:S(2)}, u32[]{:S(2)}) collective-permute-start(f32[2,3,2,1024]{3,2,1,0:T(2,128)S(1)} %get-tuple-element.31), channel_id=1, source_target_pairs={{0,16},{16,32},{32,48},{48,64},{64,80},{80,96},{96,112},{112,128},... | collective-permute-start | bytes 147464 | tf_op jit(solution)/shard_map/ppermute | solution.py:12
  259.4 2.1 collective-permute-start.3
  261.6 3.7 collective-permute-done.3
  265.6 0.5 fusion.35
  266.1 3.4 slice.404
  269.5 0.7 fusion.80
  270.2 1.9 collective-permute-start.6
  272.1 3.0 collective-permute-start.7
  275.2 0.6 copy.442
  275.8 2.5 multiply_bitcast_fusion.2
  278.3 0.7 pad_maximum_fusion.3
  279.1 6.5 copy.445
  285.6 5.5 copy.446
  291.1 78.2 %all-gather.3.cloned.1.call-done = f32[512,2048]{1,0:T(8,128)} async-done(((f32[32,2048]{1,0:T(8,128)}), f32[512,2048]{1,0:T(8,128)}) %all-gather.3.cloned.1.call-update) | async-done | bytes 4194320 | tf_op jit(solution)/shard_map/all_gather | solution.py:113
  369.3 2.5 reduce_sum.46
  371.9 4.3 collective-permute-start.4
  376.3 2.1 collective-permute-start.5
  378.4 0.9 fusion.29
  379.3 2.2 collective-permute-done.5
  381.5 0.4 broadcast_multiply_fusion.1
  381.9 1.4 add_multiply_fusion.1
  383.3 6.0 slice.397
  389.4 0.9 slice_bitcast_fusion.3
  390.2 1.9 collective-permute-start.8
  392.2 2.5 collective-permute-start.9
  394.7 2.4 multiply_reduce_fusion
  397.7 1.1 slice.421
  398.9 1.1 fusion.69
  400.2 0.7 multiply_bitcast_fusion.8
  401.1 99.0 %psum.23 = f32[1,3,8,512]{2,3,1,0:T(8,128)} all-reduce(f32[1,3,8,512]{2,3,1,0:T(8,128)S(1)} %bitcast.86), channel_id=1, replica_groups=mesh['rows'=32,'gz'=16] {'gz'}, use_global_device_ids=true, to_apply=%region_9.10 | all-reduce | flops 12288 | bytes 98304 | tf_op jit(solution)/shard_map/psum | solution.py:127
  500.1 0.9 pad_maximum_fusion.13
  501.1 3.5 copy.454
  504.6 1.8 copy.455
  506.4 1.9 multiply_reduce_fusion.1
  508.8 14.1 %collective-permute-start.10 = (f32[1,3,2,512]{3,2,1,0:T(2,128)S(1)}, f32[1,3,2,512]{3,2,1,0:T(2,128)S(1)}, u32[]{:S(2)}, u32[]{:S(2)}) collective-permute-start(f32[1,3,2,512]{3,2,1,0:T(2,128)S(1)} %copy.465), channel_id=1, source_target_pairs={{0,16},{16,32},{32,48},{48,64},{64,80},{80,96},{96,112},{112,128},... | collective-permute-start | bytes 36872 | tf_op jit(solution)/shard_map/ppermute | solution.py:12
  523.2 2.9 collective-permute-start.11
  526.4 1.8 collective-permute-done.11
  528.5 0.9 fusion.11
  529.5 0.4 copy.469
  530.0 0.7 multiply_bitcast_fusion.10
  530.9 0.8 copy.471
  531.6 0.4 copy.472
  532.1 189.7 %all-reduce.16.cloned.1.call-done = (f32[1,3,32,2048]{3,2,1,0:T(8,128)}, f32[1,3,16,1024]{3,2,1,0:T(8,128)}) async-done(((f32[1,3,32,2048]{3,2,1,0:T(8,128)}, f32[1,3,16,1024]{3,2,1,0:T(8,128)}), (f32[1,3,32,2048]{3,2,1,0:T(8,128)}, f32[1,3,16,1024]{3,2,1,0:T(8,128)})) %all-reduce.16.cloned.1.call-update) | async-done | bytes 983056 | tf_op jit(solution)/shard_map/psum | solution.py:127
  721.7 0.9 add.340
  722.7 13.3 %collective-permute-start.12 = (f32[1,3,2,1024]{3,2,1,0:T(2,128)S(1)}, f32[1,3,2,1024]{3,2,1,0:T(2,128)S(1)}, u32[]{:S(2)}, u32[]{:S(2)}) collective-permute-start(f32[1,3,2,1024]{3,2,1,0:T(2,128)S(1)} %get-tuple-element.35), channel_id=1, source_target_pairs={{0,16},{16,32},{32,48},{48,64},{64,80},{80,96},{96,112},{112,128},... | collective-permute-start | bytes 73736 | tf_op jit(solution)/shard_map/ppermute | solution.py:12
  736.0 1.9 collective-permute-start.13
  737.9 3.2 collective-permute-done.13
  741.7 2.5 multiply_bitcast_fusion.4
  744.2 1.7 pad_maximum_fusion.8
  745.8 3.7 copy.475
  749.5 1.9 copy.476
  751.4 2.3 add_bitcast_fusion
  (62 shorter events, 5.9 us)
Async XLA Ops:
  6.5 215.0 %all-reduce.14.cloned.1.call-start = ((), (), s32[]{:S(2)}) async-start(), calls=%async_computation | async-start | bytes 524288 | tf_op jit(solution)/shard_map/pmax | solution.py:110
  8.4 10.9 %collective-permute-start.1 = (f32[2,3,5,2048]{3,0,2,1:T(2,128)S(1)}, f32[2,3,5,2048]{3,0,2,1:T(2,128)S(1)}, u32[]{:S(2)}, u32[]{:S(2)}) collective-permute-start(f32[2,3,5,2048]{3,0,2,1:T(2,128)S(1)} %copy.435), channel_id=1, source_target_pairs={{16,0},{32,16},{48,32},{64,48},{80,64},{96,80},{112,96},{128,112},... | collective-permute-start | bytes 737288 | tf_op jit(solution)/shard_map/ppermute | solution.py:15
  17.4 5.0 collective-permute-start
  22.6 0.7 copy-start.5
  24.3 0.7 copy-start.8
  24.9 198.6 %copy-start = (s32[2,3,32,2048]{3,2,1,0:T(8,128)S(1)}, s32[2,3,32,2048]{3,2,1,0:T(8,128)}, u32[]{:S(2)}) copy-start(s32[2,3,32,2048]{3,2,1,0:T(8,128)} %param.2) | copy-start | bytes 4718596
  27.6 341.6 %all-gather.3.cloned.1.call-start = ((), (), s32[]{:S(2)}) async-start(), calls=%async_computation.1 | async-start | bytes 4456448 | tf_op jit(solution)/shard_map/all_gather | solution.py:113
  223.5 498.3 %all-reduce.16.cloned.1.call-start = ((), (), s32[]{:S(2)}) async-start(), calls=%async_computation.2 | async-start | bytes 1966080 | tf_op jit(solution)/shard_map/psum | solution.py:127
  245.1 16.4 %collective-permute-start.2 = (f32[2,3,2,1024]{3,2,1,0:T(2,128)S(1)}, f32[2,3,2,1024]{3,2,1,0:T(2,128)S(1)}, u32[]{:S(2)}, u32[]{:S(2)}) collective-permute-start(f32[2,3,2,1024]{3,2,1,0:T(2,128)S(1)} %get-tuple-element.31), channel_id=1, source_target_pairs={{0,16},{16,32},{32,48},{48,64},{64,80},{80,96},{96,112},{112,128},... | collective-permute-start | bytes 147464 | tf_op jit(solution)/shard_map/ppermute | solution.py:12
  259.4 5.8 collective-permute-start.3
  269.5 6.3 copy-start.7
  270.2 128.6 %collective-permute-start.6 = (f32[2,3,2,512]{3,2,1,0:T(2,128)}, f32[2,3,2,512]{3,2,1,0:T(2,128)}, u32[]{:S(2)}, u32[]{:S(2)}) collective-permute-start(f32[2,3,2,512]{3,2,1,0:T(2,128)} %get-tuple-element.46), channel_id=1, source_target_pairs={{0,16},{16,32},{32,48},{48,64},{64,80},{80,96},{96,112},{112,128},... | collective-permute-start | bytes 73736 | tf_op jit(solution)/shard_map/ppermute | solution.py:12
  272.1 126.7 %collective-permute-start.7 = (f32[2,3,2,512]{3,2,1,0:T(2,128)}, f32[2,3,2,512]{3,2,1,0:T(2,128)}, u32[]{:S(2)}, u32[]{:S(2)}) collective-permute-start(f32[2,3,2,512]{3,2,1,0:T(2,128)} %get-tuple-element.47), channel_id=1, source_target_pairs={{16,0},{32,16},{48,32},{64,48},{80,64},{96,80},{112,96},{128,112},... | collective-permute-start | bytes 73736 | tf_op jit(solution)/shard_map/ppermute | solution.py:15
  369.3 2.5 copy-start.1
  369.3 2.5 copy-start.4
  371.9 7.4 collective-permute-start.4
  376.3 5.2 collective-permute-start.5
  381.9 12.8 %copy-start.3 = (f32[2,3,32,2048]{3,2,1,0:T(8,128)S(1)}, f32[2,3,32,2048]{3,2,1,0:T(8,128)}, u32[]{:S(2)}) copy-start(f32[2,3,32,2048]{3,2,1,0:T(8,128)} %copy.446) | copy-start | bytes 4718596
  390.2 6.9 collective-permute-start.8
  392.2 5.2 copy-start.6
  392.2 5.2 collective-permute-start.9
  506.4 1.9 copy-start.2
  508.8 17.3 %collective-permute-start.10 = (f32[1,3,2,512]{3,2,1,0:T(2,128)S(1)}, f32[1,3,2,512]{3,2,1,0:T(2,128)S(1)}, u32[]{:S(2)}, u32[]{:S(2)}) collective-permute-start(f32[1,3,2,512]{3,2,1,0:T(2,128)S(1)} %copy.465), channel_id=1, source_target_pairs={{0,16},{16,32},{32,48},{48,64},{64,80},{80,96},{96,112},{112,128},... | collective-permute-start | bytes 36872 | tf_op jit(solution)/shard_map/ppermute | solution.py:12
  523.2 5.0 collective-permute-start.11
  722.7 15.2 %collective-permute-start.12 = (f32[1,3,2,1024]{3,2,1,0:T(2,128)S(1)}, f32[1,3,2,1024]{3,2,1,0:T(2,128)S(1)}, u32[]{:S(2)}, u32[]{:S(2)}) collective-permute-start(f32[1,3,2,1024]{3,2,1,0:T(2,128)S(1)} %get-tuple-element.35), channel_id=1, source_target_pairs={{0,16},{16,32},{32,48},{48,64},{64,80},{80,96},{96,112},{112,128},... | collective-permute-start | bytes 73736 | tf_op jit(solution)/shard_map/ppermute | solution.py:12
  736.0 5.1 collective-permute-start.13
Sparse Core Ops, SparseCore 0:
  27.7 193.7 all-reduce.13
  225.0 144.2 all-gather.2
  508.4 213.2 all-reduce.15
